TPU v7x, 32 devices: a whole 2x2x4 slice. The times are simulated.
32 devices in a mesh: tm: 4 (over z), expert: 8 (over y, x, core).
Axes of the slice: x: 2, y: 2, z: 4, core: 2. Of those that a mesh axis runs over, the one named last changes fastest.
Arguments:
- x_in: float32 [8, 1024, 1024], P('expert', 'tm'), may hold values from -6 to 6
- z_gate: bfloat16 [8, 1024, 1024], P('expert', 'tm'), may hold values from -6 to 6
- b_proj: float32 [8, 1024, 128], P('expert', 'tm'), may hold values from -1.5 to 1.5
- c_proj: float32 [8, 1024, 128], P('expert', 'tm'), may hold values from -1.5 to 1.5
- decay_log: float32 [8, 1024, 16], P('expert', 'tm'), as said below
- skip_gain: float32 [16], replicated, may hold values from 0.5 to 2
- residual: float32 [8, 1024, 1024], P('expert', 'tm'), may hold values from -6 to 6
- ssd_gain: float32 [1024], replicated, may hold values from 0.5 to 1.5
- moe_gain: float32 [1024], replicated, may hold values from 0.5 to 1.5
- w_gate: bfloat16 [8, 1024, 1536], P('expert', 'tm'), may hold values from -0.1875 to 0.1875
- w_up: bfloat16 [8, 1024, 1536], P('expert', 'tm'), may hold values from -0.1875 to 0.1875
- w_down: bfloat16 [8, 1536, 1024], P('expert', 'tm'), may hold values from -0.15625 to 0.15625
- routes: int32 [8, 1024, 2], P('expert', 'tm'), may hold values from 0 to 7, all different within a row; in each aligned block of 256 rows (0 to 255, 256 to 511, ..., all dimensions but the last counted through in order) at most 96 rows name the same one
- route_weights: float32 [8, 1024, 2], P('expert', 'tm'), may hold values from 0.2 to 1
Outputs:
- mixed: float32 [8, 1024, 1024], P('expert', 'tm')
Inputs may be any that keep to these rules, and one draw needn't show every extreme that they name: `routes`: the two experts of a time step differ. Among the time steps of one device no expert is named more than 96 times, and in every draw some device names some expert exactly 96 times. `decay_log`: every entry is at most zero.
All inputs are finite; a program needn't handle non-finite values.
Results may differ from a plain program's by a relative error of at most 0.0021.
Values may be sent and summed in bfloat16 or wider, within the bound.
A program may use at most 64 MiB of HBM per device.

v0:
```python
import math

import jax
import jax.numpy as jnp
from jax import lax
from jax.sharding import PartitionSpec as P

exact_mode = lax.Precision.HIGHEST


def carried_in_2(value, axis, join, neutral):
    count, mine = (lax.axis_size(axis), lax.axis_index(axis))
    pieces = jax.tree.map(lambda part: lax.all_gather(part, axis), value)
    running = jax.tree.map(
        lambda part, zero: jnp.full_like(part, 0) + jnp.asarray(zero, part.dtype), value, neutral
    )

    def lap(position, running):
        longer = join(running, jax.tree.map(lambda part: part[position], pieces))
        return jax.tree.map(lambda new, old: jnp.where(position < mine, new, old), longer, running)

    return lax.fori_loop(0, count - 1, lap, running)


def group_carry(state, values, b_rows, running):
    remains = jnp.exp(running[-1][None, :] - running)
    fresh = jnp.einsum("jhp,jn->hpn", values * remains[:, :, None], b_rows, precision=exact_mode)
    return jnp.exp(running[-1])[:, None, None] * state + fresh


def group_step(state, inputs, skip_gain):
    values, b_rows, c_rows, log_rates = inputs
    length = values.shape[0]
    running = jnp.cumsum(log_rates, axis=0)
    across = running.T[:, :, None] - running.T[:, None, :]
    places = jnp.arange(length)
    causal = (places[:, None] >= places[None, :])[None]
    masked = jnp.where(causal, jnp.exp(jnp.where(causal, across, 0.0)), 0.0)
    scores = jnp.dot(c_rows, b_rows.T, precision=exact_mode)
    mixing = masked * scores[None]
    output = jnp.einsum("hij,jhp->ihp", mixing, values, precision=exact_mode)
    output = output + jnp.exp(running)[:, :, None] * jnp.einsum(
        "in,hpn->ihp", c_rows, state, precision=exact_mode
    )
    output = output + skip_gain[None, :, None] * values
    return (group_carry(state, values, b_rows, running), output)


def incoming_state(through, local_end):

    def combine(earlier, later):
        return (earlier[0] * later[0], later[0][:, None, None] * earlier[1] + later[1])

    prefix = carried_in_2(
        (through, local_end), "tm", combine, (jnp.ones_like(through), jnp.zeros_like(local_end))
    )
    return prefix[1]


def rms_scale(rows, gain):
    return gain * rows / jnp.sqrt(jnp.mean(rows * rows, axis=-1, keepdims=True) + 1e-05)


def per_device(
    x_in,
    z_gate,
    b_proj,
    c_proj,
    decay_log,
    skip_gain,
    residual,
    ssd_gain,
    moe_gain,
    w_gate,
    w_up,
    w_down,
    routes,
    route_weights,
):
    heads = skip_gain.shape[0]
    model_width = x_in.shape[2]
    width = model_width // heads
    length = x_in.shape[1]
    block = math.gcd(length, 256)
    count = length // block
    values = x_in[0].reshape(length, heads, width)
    b_rows = b_proj[0]
    c_rows = c_proj[0]
    log_rates = decay_log[0]
    inputs = (
        values.reshape(count, block, heads, width),
        b_rows.reshape(count, block, -1),
        c_rows.reshape(count, block, -1),
        log_rates.reshape(count, block, heads),
    )
    start = jnp.zeros((heads, width, b_rows.shape[1]), jnp.float32)
    through = jnp.exp(jnp.sum(log_rates, axis=0))
    local_end, outputs = lax.scan(
        lambda state, piece: group_step(state, piece, skip_gain), start, inputs
    )
    incoming = incoming_state(through, local_end)
    running = jnp.cumsum(log_rates, axis=0)
    carried_in = jnp.exp(running)[:, :, None] * jnp.einsum(
        "in,hpn->ihp", c_rows, incoming, precision=exact_mode
    )
    mixed_ssd = (outputs.reshape(length, heads, width) + carried_in).reshape(length, model_width)
    gated = mixed_ssd * jax.nn.silu(z_gate[0].astype(jnp.float32))
    hres = residual[0] + rms_scale(gated, ssd_gain)
    normed = rms_scale(hres, moe_gain).astype(jnp.bfloat16)
    expert_count = lax.axis_size("expert")
    capacity = max(2, 3 * length // expert_count)
    flat_routes = routes[0].reshape(-1)
    picked_one = (flat_routes[:, None] == jnp.arange(expert_count)[None, :]).astype(jnp.int32)
    earlier_hits = jnp.cumsum(picked_one, axis=0) - picked_one
    slot_index = jnp.sum(earlier_hits * picked_one, axis=1)
    target = flat_routes * capacity + slot_index
    repeated = jnp.broadcast_to(normed[:, None, :], (length, 2, model_width)).reshape(
        2 * length, model_width
    )
    outgoing = (
        jnp.zeros((expert_count * capacity, model_width), jnp.bfloat16).at[target].set(repeated)
    )
    received = lax.all_to_all(
        outgoing.reshape(expert_count, capacity, model_width),
        "expert",
        split_axis=0,
        concat_axis=0,
        tiled=True,
    )
    received = received.reshape(expert_count * capacity, model_width)
    slot_rows = expert_count * capacity
    columns = received
    gate = jnp.dot(
        columns,
        lax.all_gather(w_gate[0], "tm", axis=0, tiled=True),
        preferred_element_type=jnp.float32,
    )
    upper = jnp.dot(
        columns,
        lax.all_gather(w_up[0], "tm", axis=0, tiled=True),
        preferred_element_type=jnp.float32,
    )
    hidden = (jax.nn.silu(gate) * upper).astype(jnp.bfloat16)
    columns = hidden
    produced = jnp.dot(
        columns,
        lax.all_gather(w_down[0], "tm", axis=0, tiled=True),
        preferred_element_type=jnp.float32,
    ).astype(jnp.bfloat16)
    back = lax.all_to_all(
        produced.reshape(expert_count, capacity, model_width),
        "expert",
        split_axis=0,
        concat_axis=0,
        tiled=True,
    )
    back = back.reshape(slot_rows, model_width)
    fetched = back[target].astype(jnp.float32).reshape(length, 2, model_width)
    weights_here = route_weights[0]
    moe = fetched[:, 0, :] * weights_here[:, 0:1] + fetched[:, 1, :] * weights_here[:, 1:2]
    return (hres + moe).reshape(1, length, model_width)


def solution(mesh):
    in_specs = (
        P("expert", "tm", None),
        P("expert", "tm", None),
        P("expert", "tm", None),
        P("expert", "tm", None),
        P("expert", "tm", None),
        P(),
        P("expert", "tm", None),
        P(),
        P(),
        P("expert", "tm", None),
        P("expert", "tm", None),
        P("expert", "tm", None),
        P("expert", "tm", None),
        P("expert", "tm", None),
    )
    out_specs = P("expert", "tm", None)
    return jax.shard_map(
        per_device, mesh=mesh, in_specs=in_specs, out_specs=out_specs, check_vma=False
    )
```

profile of v0, /device:TPU:0, one launch (start us, length us, event | category | flops | bytes accessed | tf_op | source)
XLA Modules:
  0.0 302.3 jit_solution(10193187537252534678)
XLA Ops:
  8.4 1.6 copy.52
  10.2 1.8 convolution_add_fusion
  16.4 13.8 %all-reduce = f32[64]{0:T(128)S(1)} all-reduce(f32[64]{0:T(128)S(1)} %exponential_dynamic-update-slice_fusion), channel_id=2, replica_groups=mesh['tm'=4,'expert'=8] {'tm'}, use_global_device_ids=true, to_apply=%add | all-reduce | flops 64 | bytes 512
  33.3 5.1 %fusion.24 = f32[256,16,64]{0,2,1:T(8,128)S(1)} fusion(f32[256,16,64]{0,2,1:T(8,128)S(1)} %bitcast.150, f32[256,256]{1,0:T(8,128)S(1)} %fusion.49, f32[16,256]{1,0:T(8,128)S(1)} %get-tuple-element.159, pred[256,256]{1,0:T(8,128)(4,1)S(1)} %iota_compare_fusion), kind=kOutput, calls=%fused_computation.23 | convolution fusion | flops 809500672 | bytes 2441216 | tf_op jit(solution)/shard_map/while/body/eval_jaxpr/hij,jhp->ihp/dot_general | solution.py:41
  38.4 2.0 fusion.31
  40.5 20.3 %all-gather.10.cloned.1.call-done = f32[64,64,128]{2,1,0:T(8,128)} async-done(((f32[16,64,128]{2,1,0:T(8,128)}), f32[64,64,128]{2,1,0:T(8,128)}) %all-gather.10.cloned.1.call-update) | async-done | bytes 2097168 | tf_op jit(solution)/shard_map/all_gather | solution.py:13
  60.8 3.6 %while.9 = (s32[]{:T(128)}, f32[16,64,128]{2,1,0:T(8,128)S(1)}, s32[]{:T(128)}, f32[4,16]{1,0:T(4,128)S(1)}, f32[4,16,64,128]{3,2,1,0:T(8,128)}, /*index=5*/s32[]{:T(128)}, s32[]{:T(128)}) while((s32[]{:T(128)}, f32[16,64,128]{2,1,0:T(8,128)S(1)}, s32[]{:T(128)}, f32[4,16]{1,0:T(4,128)S(1)}, f32[4,16,64,128]{3,2,1,0:T(8,128)}, ...), condition=%wide.region_4.5_spmd.clone, body=%wide.region_3.4_spmd.clone.sunk | while | flops 524292 | bytes 1573161 | solution.py:22
  64.5 2.8 multiply_reduce_fusion.1
  67.3 1.3 copy.59
  68.6 1.8 multiply_reduce_fusion
  72.4 3.7 %scatter_custom_fusion = bf16[768,1024]{1,0:T(8,128)(2,1)S(1)} fusion(s32[512]{0:T(512)S(1)} %bitcast.161, bf16[512,1024]{1,0:T(8,128)(2,1)} %reshape.351, bf16[]{:T(256)} %constant.71.clone.1), kind=kCustom, calls=%fused_computation.51 | custom fusion | bytes 1573376 | tf_op jit(solution)/shard_map/scatter | solution.py:121
  76.1 24.6 %all_to_all.10 = bf16[8,96,1024]{2,1,0:T(8,128)(2,1)} all-to-all(bf16[8,96,1024]{2,1,0:T(8,128)(2,1)S(1)} %bitcast.152), channel_id=1, replica_groups=mesh['tm'=4,'expert'=8] {'expert'}, dimensions={0} | all-to-all | bytes 3145728 | tf_op jit(solution)/shard_map/all_to_all | solution.py:123
  100.7 24.0 %all-gather.12.cloned.1.call-done = bf16[1,1024,1536]{2,1,0:T(8,128)(2,1)} async-done(((bf16[1,256,1536]{2,1,0:T(8,128)(2,1)}), bf16[1,1024,1536]{2,1,0:T(8,128)(2,1)}) %all-gather.12.cloned.1.call-update) | async-done | bytes 3145744 | tf_op jit(solution)/shard_map/all_gather | solution.py:135
  124.7 7.2 %fusion.10 = f32[768,1536]{1,0:T(8,128)} fusion(bf16[768,1024]{1,0:T(8,128)(2,1)} %bitcast.158, bf16[1,1024,1536]{2,1,0:T(8,128)(2,1)} %all-gather.12.cloned.1.call-done), kind=kOutput, calls=%fused_computation.15 | convolution fusion | flops 2415919104 | bytes 9437184 | tf_op jit(solution)/shard_map/dot_general | solution.py:133
  131.9 56.6 %all-gather.14.cloned.1.call-done = bf16[1,1024,1536]{2,1,0:T(8,128)(2,1)} async-done(((bf16[1,256,1536]{2,1,0:T(8,128)(2,1)}), bf16[1,1024,1536]{2,1,0:T(8,128)(2,1)}) %all-gather.14.cloned.1.call-update) | async-done | bytes 3145744 | tf_op jit(solution)/shard_map/all_gather | solution.py:140
  188.4 63.6 %all-gather.16.cloned.1.call-done = bf16[1,1536,1024]{2,1,0:T(8,128)(2,1)} async-done(((bf16[1,384,1024]{2,1,0:T(8,128)(2,1)}), bf16[1,1536,1024]{2,1,0:T(8,128)(2,1)}) %all-gather.16.cloned.1.call-update) | async-done | bytes 3145744 | tf_op jit(solution)/shard_map/all_gather | solution.py:147
  252.1 10.4 %fusion.19 = bf16[768,1024]{1,0:T(8,128)(2,1)} fusion(bf16[1,1536,1024]{2,1,0:T(8,128)(2,1)} %all-gather.16.cloned.1.call-done, f32[768,1536]{1,0:T(8,128)} %fusion.10, bf16[768,1024]{1,0:T(8,128)(2,1)S(1)} %bitcast.159, bf16[1,1024,1536]{2,1,0:T(8,128)(2,1)} %all-gather.14.cloned.1.call-done), kind=kOutput, calls=%fused_computation.22 | convolution fusion | flops 4839702528 | bytes 14155776 | tf_op jit(solution)/shard_map/dot_general | solution.py:145
  262.5 3.8 %all-to-all-start.1 = ((bf16[8,96,1024]{2,1,0:T(8,128)(2,1)}), bf16[8,96,1024]{2,1,0:T(8,128)(2,1)S(1)}, u32[]{:S(2)}, u32[]{:S(2)}) async-start(bf16[8,96,1024]{2,1,0:T(8,128)(2,1)} %bitcast.157), calls=%async_computation.1 | async-start | bytes 3145728 | tf_op jit(solution)/shard_map/all_to_all | solution.py:150
  266.3 1.3 copy.54
  267.6 19.7 %all-to-all-done.1 = bf16[8,96,1024]{2,1,0:T(8,128)(2,1)S(1)} async-done(((bf16[8,96,1024]{2,1,0:T(8,128)(2,1)}), bf16[8,96,1024]{2,1,0:T(8,128)(2,1)S(1)}, u32[]{:S(2)}, u32[]{:S(2)}) %all-to-all-start.1) | async-done | bytes 1572896 | tf_op jit(solution)/shard_map/all_to_all | solution.py:150
  287.3 2.8 gather_fusion
  290.1 2.4 reshape.338
  292.5 1.6 fusion.60
  294.1 1.6 fusion.34
  (81 shorter events, 14.2 us)
Async XLA Ops:
  6.5 8.1 %copy-start = (f32[1,256,128]{2,1,0:T(8,128)S(1)}, f32[1,256,128]{2,1,0:T(8,128)}, u32[]{:S(2)}) copy-start(f32[1,256,128]{2,1,0:T(8,128)} %param.19) | copy-start | bytes 393220
  6.5 3.6 %copy-start.6 = (f32[1,256,128]{2,1,0:T(8,128)S(1)}, f32[1,256,128]{2,1,0:T(8,128)}, u32[]{:S(2)}) copy-start(f32[1,256,128]{2,1,0:T(8,128)} %param.18) | copy-start | bytes 393220
  6.5 54.3 %all-gather.10.cloned.1.call-start = ((), (), s32[]{:S(2)}) async-start(), calls=%async_computation.2 | async-start | bytes 2621440 | tf_op jit(solution)/shard_map/all_gather | solution.py:13
  10.0 4.1 %copy-start.7 = (f32[1,256,16]{1,2,0:T(8,128)S(1)}, f32[1,256,16]{1,2,0:T(8,128)}, u32[]{:S(2)}) copy-start(f32[1,256,16]{1,2,0:T(8,128)} %param.20) | copy-start | bytes 49156
  10.0 4.2 %copy-start.9 = (s32[1,256,2]{1,2,0:T(2,128)S(1)}, s32[1,256,2]{1,2,0:T(2,128)}, u32[]{:S(2)}) copy-start(s32[1,256,2]{1,2,0:T(2,128)} %param.28) | copy-start | bytes 6148
  10.1 4.9 %copy-start.13 = (u32[32]{0:T(128)S(1)}, u32[32]{0:T(128)}, u32[]{:S(2)}) copy-start(u32[32]{0:T(128)} %constant.87) | copy-start | bytes 388
  10.1 20.2 %copy-start.1 = (bf16[1,256,1024]{2,1,0:T(8,128)(2,1)S(1)}, bf16[1,256,1024]{2,1,0:T(8,128)(2,1)}, u32[]{:S(2)}) copy-start(bf16[1,256,1024]{2,1,0:T(8,128)(2,1)} %param.17) | copy-start | bytes 1572868
  12.0 112.7 %all-gather.12.cloned.1.call-start = ((), (), s32[]{:S(2)}) async-start(), calls=%async_computation.3 | async-start | bytes 3932160 | tf_op jit(solution)/shard_map/all_gather | solution.py:135
  12.7 175.7 %all-gather.14.cloned.1.call-start = ((), (), s32[]{:S(2)}) async-start(), calls=%async_computation.4 | async-start | bytes 3932160 | tf_op jit(solution)/shard_map/all_gather | solution.py:140
  13.4 238.6 %all-gather.16.cloned.1.call-start = ((), (), s32[]{:S(2)}) async-start(), calls=%async_computation.5 | async-start | bytes 3932160 | tf_op jit(solution)/shard_map/all_gather | solution.py:147
  33.3 5.1 %copy-start.12 = (f32[16]{0:T(128)S(1)}, f32[16]{0:T(128)}, u32[]{:S(2)}) copy-start(f32[16]{0:T(128)} %param.21) | copy-start | bytes 196
  64.4 4.2 %copy-start.3 = (f32[1,256,1024]{2,1,0:T(8,128)S(1)}, f32[1,256,1024]{2,1,0:T(8,128)}, u32[]{:S(2)}) copy-start(f32[1,256,1024]{2,1,0:T(8,128)} %param.22) | copy-start | bytes 3145732
  64.4 4.2 %copy-start.8 = (f32[1024]{0:T(1024)S(1)}, f32[1024]{0:T(1024)}, u32[]{:S(2)}) copy-start(f32[1024]{0:T(1024)} %param.23) | copy-start | bytes 12292
  67.3 3.2 %copy-start.10 = (f32[1024]{0:T(1024)S(1)}, f32[1024]{0:T(1024)}, u32[]{:S(2)}) copy-start(f32[1024]{0:T(1024)} %param.24) | copy-start | bytes 12292
  124.7 127.4 %copy-start.5 = (bf16[8,96,1024]{2,1,0:T(8,128)(2,1)S(1)}, bf16[8,96,1024]{2,1,0:T(8,128)(2,1)}, u32[]{:S(2)}) copy-start(bf16[8,96,1024]{2,1,0:T(8,128)(2,1)} %all_to_all.10) | copy-start | bytes 4718596
  262.5 3.8 %copy-start.11 = (f32[1,256,2]{1,2,0:T(2,128)S(1)}, f32[1,256,2]{1,2,0:T(2,128)}, u32[]{:S(2)}) copy-start(f32[1,256,2]{1,2,0:T(2,128)} %param.29) | copy-start | bytes 6148
  262.5 24.8 %all-to-all-start.1 = ((bf16[8,96,1024]{2,1,0:T(8,128)(2,1)}), bf16[8,96,1024]{2,1,0:T(8,128)(2,1)S(1)}, u32[]{:S(2)}, u32[]{:S(2)}) async-start(bf16[8,96,1024]{2,1,0:T(8,128)(2,1)} %bitcast.157), calls=%async_computation.1 | async-start | bytes 3145728 | tf_op jit(solution)/shard_map/all_to_all | solution.py:150
  292.4 1.7 copy-start.2
  292.4 1.7 copy-start.4
Sparse Core Ops, SparseCore 0:
  12.1 48.6 all-gather.9
  62.4 62.2 all-gather.11
  126.3 62.1 all-gather.13
  189.9 62.1 all-gather.15
where the time goes:
time: 303 us; the launch traced here: 302 us
  waiting for transfers between devices  186 us (61%)
  blocking collectives  38.4 us (13%)
  matrix products  29.7 us (10%)
  local copies, waits for them, and re-layouts  20.5 us (7%)
  between operations  14.1 us (5%)
  other arithmetic  9.45 us (3%)
  starting transfers between devices  3.91 us (1%)
    all_gather x1, waiting for transfers between devices, per_device(): lax.all_gather(w_down[0], 'tm', axis=0, tiled=True)  63.6 us
    all_gather x1, waiting for transfers between devices, per_device(): lax.all_gather(w_up[0], 'tm', axis=0, tiled=True)  56.6 us
    all_to_all x1, blocking collectives, per_device(): lax.all_to_all(outgoing.reshape(expert_count, capacity, model_width), 'ex...  24.6 us
    all_gather x1, waiting for transfers between devices, per_device(): lax.all_gather(w_gate[0], 'tm', axis=0, tiled=True)  24 us
    all_gather x1, waiting for transfers between devices, carried_in_2(): pieces = jax.tree.map(lambda part: lax.all_gather(part, axis), value)  20.3 us
    all_to_all x1, waiting for transfers between devices, per_device(): lax.all_to_all(produced.reshape(expert_count, capacity, model_width), 'ex...  19.7 us
    unnamed x1, blocking collectives  13.8 us
    dot_general x1, matrix products, per_device(): jnp.dot(columns, lax.all_gather(w_down[0], 'tm', axis=0, tiled=True), pre...  10.4 us
  transfers between devices with their start and end apart: 5, of which 5 were waited for; matrix products, arithmetic and copies ran while one was open for 12% of the time, Pallas kernels for 0%

commit v1 on v0

v1 whole, which is shorter than its diff:
```python
import jax
import jax.numpy as jnp
from jax import lax
from jax.sharding import Mesh
from jax.sharding import PartitionSpec as P

exact_mode = lax.Precision.HIGHEST

TM = ("zh", "zp")
EXPERT = ("col", "core")


def state_before(through, local_end):
    count = lax.axis_size(TM)

    def shifted(value, by):
        pairs = [(z, z + by) for z in range(count - by)]
        return lax.ppermute(value, TM, pairs)

    decay = shifted(through, 1)
    state = shifted(local_end.astype(jnp.bfloat16), 1).astype(jnp.float32)
    by = 1
    while by < count - 1:
        earlier = shifted(state.astype(jnp.bfloat16), by).astype(jnp.float32)
        state = decay[:, None, None] * earlier + state
        if 2 * by < count - 1:
            decay = decay * shifted(decay, by)
        by *= 2
    return state


def whole_expert(shard, exchange_axes):
    count = lax.axis_size(TM)
    place = lax.axis_index(TM)
    core = lax.axis_index("core")
    group = lax.axis_index("zh")
    rows, width = shard.shape
    half = rows // 2
    halves = shard.reshape(2, half, width)
    full = jnp.zeros((count, 2, half, width), shard.dtype)
    for turn in range(count):
        pairs = []
        for z in range(count):
            spot = (z + turn) % count
            for owned in range(2):
                pairs.append((z * 2 + owned, (owned + 2 * (spot // 2)) * 2 + spot % 2))
        wanted = lax.rem(place + turn, 2)
        piece = lax.dynamic_index_in_dim(halves, wanted, 0, keepdims=False)
        mine = lax.ppermute(piece, exchange_axes, pairs)
        other = lax.ppermute(mine, "core", [(0, 1), (1, 0)])
        origin = lax.rem(2 * group + core - turn + count, count)
        origin_other = lax.rem(2 * group + 1 - core - turn + count, count)
        full = lax.dynamic_update_slice(full, mine[None, None], (origin, core, 0, 0))
        full = lax.dynamic_update_slice(full, other[None, None], (origin_other, 1 - core, 0, 0))
    return full.reshape(count * rows, width)


def rms_scale(rows, gain):
    return gain * rows / jnp.sqrt(jnp.mean(rows * rows, axis=-1, keepdims=True) + 1e-05)


def per_device(
    x_in,
    z_gate,
    b_proj,
    c_proj,
    decay_log,
    skip_gain,
    residual,
    ssd_gain,
    moe_gain,
    w_gate,
    w_up,
    w_down,
    routes,
    route_weights,
):
    heads = skip_gain.shape[0]
    model_width = x_in.shape[2]
    width = model_width // heads
    length = x_in.shape[1]
    hidden_width = w_gate.shape[2]

    both = whole_expert(jnp.concatenate([w_gate[0], w_up[0]], axis=1), ("zh", "zp", "core"))
    down = whole_expert(w_down[0], ("zh", "zp", "core"))

    values = x_in[0].reshape(length, heads, width)
    b_rows = b_proj[0]
    c_rows = c_proj[0]
    running = jnp.cumsum(decay_log[0], axis=0)
    through = jnp.exp(running[-1])
    remains = jnp.exp(running[-1][None, :] - running)
    local_end = jnp.einsum(
        "jhp,jn->hpn", values * remains[:, :, None], b_rows, precision=exact_mode
    )
    incoming = state_before(through, local_end)

    across = running.T[:, :, None] - running.T[:, None, :]
    places = jnp.arange(length)
    causal = (places[:, None] >= places[None, :])[None]
    masked = jnp.where(causal, jnp.exp(jnp.where(causal, across, 0.0)), 0.0)
    scores = jnp.dot(c_rows, b_rows.T, precision=exact_mode)
    output = jnp.einsum("hij,jhp->ihp", masked * scores[None], values, precision=exact_mode)
    output = output + skip_gain[None, :, None] * values
    output = output + jnp.exp(running)[:, :, None] * jnp.einsum(
        "in,hpn->ihp", c_rows, incoming, precision=exact_mode
    )
    gated = output.reshape(length, model_width) * jax.nn.silu(z_gate[0].astype(jnp.float32))
    hres = residual[0] + rms_scale(gated, ssd_gain)
    normed = rms_scale(hres, moe_gain).astype(jnp.bfloat16)

    expert_count = lax.axis_size(EXPERT)
    capacity = max(2, 3 * length // expert_count)
    slot_rows = expert_count * capacity
    flat_routes = routes[0].reshape(-1)
    picked_one = (flat_routes[:, None] == jnp.arange(expert_count)[None, :]).astype(jnp.int32)
    earlier_hits = jnp.cumsum(picked_one, axis=0) - picked_one
    slot_index = jnp.sum(earlier_hits * picked_one, axis=1)
    block = (flat_routes % 2) * (expert_count // 2) + flat_routes // 2
    target = block * capacity + slot_index
    repeated = jnp.broadcast_to(normed[:, None, :], (length, 2, model_width)).reshape(
        2 * length, model_width
    )
    outgoing = jnp.zeros((slot_rows, model_width), jnp.bfloat16).at[target].set(repeated)
    received = lax.all_to_all(
        outgoing.reshape(expert_count, capacity, model_width),
        ("zp", "col"),
        split_axis=0,
        concat_axis=0,
        tiled=True,
    ).reshape(slot_rows, model_width)
    gate_up = jnp.dot(received, both, preferred_element_type=jnp.float32)
    hidden = (jax.nn.silu(gate_up[:, :hidden_width]) * gate_up[:, hidden_width:]).astype(
        jnp.bfloat16
    )
    produced = jnp.dot(hidden, down, preferred_element_type=jnp.float32).astype(jnp.bfloat16)
    back = lax.all_to_all(
        produced.reshape(expert_count, capacity, model_width),
        ("zp", "col"),
        split_axis=0,
        concat_axis=0,
        tiled=True,
    ).reshape(slot_rows, model_width)
    fetched = back[target].astype(jnp.float32).reshape(length, 2, model_width)
    weights_here = route_weights[0]
    moe = fetched[:, 0, :] * weights_here[:, 0:1] + fetched[:, 1, :] * weights_here[:, 1:2]
    return (hres + moe).reshape(1, length, model_width)


def solution(mesh):
    tm, expert = mesh.shape["tm"], mesh.shape["expert"]
    finer = Mesh(
        mesh.devices.reshape(tm // 2, 2, expert // 2, 2), ("zh", "zp", "col", "core")
    )
    split = P(EXPERT, TM, None)
    in_specs = tuple(P() if place in (5, 7, 8) else split for place in range(14))
    return jax.shard_map(
        per_device, mesh=finer, in_specs=in_specs, out_specs=split, check_vma=False
    )
```

time: 303 us -> 218 us (0.72)
  waiting for transfers between devices: 186 us -> 65.7 us
  starting transfers between devices: 3.91 us -> 75.3 us
  blocking collectives: 38.4 us -> 0 us
  local copies, waits for them, and re-layouts: 20.5 us -> 43 us
  between operations: 14.1 us -> 0.55 us
  matrix products: 29.7 us -> 21.7 us
    all_gather x4 -> x0, waiting for transfers between devices: 165 us -> none  [the longest x1 63.6 us: per_device(): lax.all_gather(w_down[0], 'tm', axis=0, tiled=True)]
    ppermute x0 -> x21, starting transfers between devices: none -> 66.1 us  [the longest x8 25.8 us: whole_expert(): mine = lax.ppermute(piece, exchange_axes, pairs)]
    ppermute x0 -> x21, waiting for transfers between devices: none -> 46.2 us  [the longest x8 44.4 us: whole_expert(): mine = lax.ppermute(piece, exchange_axes, pairs)]
    all_to_all x1 -> x0, blocking collectives: 24.6 us -> none  [per_device(): lax.all_to_all(outgoing.reshape(expert_count, capacity, model_width), 'ex...]
    dynamic_update_slice x0 -> x16, local copies, waits for them, and re-layouts: none -> 19.2 us  [the longest x8 11.3 us: whole_expert(): lax.dynamic_update_slice(full, mine[None, None], (origin, core, 0, 0))]
    unnamed x1 -> x0, blocking collectives: 13.8 us -> none
    dot_general x6 -> x5, matrix products: 26.9 us -> 18.7 us  [the longest x1 7.26 us: per_device(): gate_up = jnp.dot(received, both, preferred_element_type=jnp.float32)]
    all_to_all x1 -> x2, starting transfers between devices: 3.79 us -> 9.11 us  [the longest x1 5.18 us: per_device(): lax.all_to_all(outgoing.reshape(expert_count, capacity, model_width), ('z...]
  transfers between devices with their start and end apart: 5 -> 23, of which waited for: 5 -> 5; matrix products, arithmetic and copies ran while one was open for 12% -> 24% of each run, Pallas kernels for 0% -> 0%
where the time goes in v1:
time: 218 us; the launch traced here: 216 us
  starting transfers between devices  75.3 us (35%)
  waiting for transfers between devices  65.7 us (30%)
  local copies, waits for them, and re-layouts  43 us (20%)
  matrix products  21.7 us (10%)
  other arithmetic  10.3 us (5%)
    ppermute x8, waiting for transfers between devices, whole_expert(): mine = lax.ppermute(piece, exchange_axes, pairs)  44.4 us
    ppermute x8, starting transfers between devices, whole_expert(): mine = lax.ppermute(piece, exchange_axes, pairs)  25.8 us
    ppermute x5, starting transfers between devices, shifted(): return lax.ppermute(value, TM, pairs)  21.9 us
    all_to_all x1, waiting for transfers between devices, per_device(): lax.all_to_all(produced.reshape(expert_count, capacity, model_width), ('z...  19.5 us
    ppermute x8, starting transfers between devices, whole_expert(): other = lax.ppermute(mine, 'core', [(0, 1), (1, 0)])  18.4 us
    dynamic_update_slice x8, local copies, waits for them, and re-layouts, whole_expert(): lax.dynamic_update_slice(full, mine[None, None], (origin, core, 0, 0))  11.3 us
    dynamic_update_slice x8, local copies, waits for them, and re-layouts, whole_expert(): lax.dynamic_update_slice(full, other[None, None], (origin_other, 1 - core...  7.88 us
    dot_general x1, matrix products, per_device(): gate_up = jnp.dot(received, both, preferred_element_type=jnp.float32)  7.26 us
  transfers between devices with their start and end apart: 23, of which 5 were waited for; matrix products, arithmetic and copies ran while one was open for 24% of the time, Pallas kernels for 0%

profile of v1, /device:TPU:0, one launch (start us, length us, event | category | flops | bytes accessed | tf_op | source)
XLA Modules:
  0.0 216.4 jit_solution(4026695874892249652)
XLA Ops:
  0.0 3.7 %fusion.37 = (bf16[128,3072]{1,0:T(8,128)(2,1)}, bf16[128,3072]{1,0:T(8,128)(2,1)}, bf16[128,3072]{1,0:T(8,128)(2,1)}, bf16[128,3072]{1,0:T(8,128)(2,1)}) fusion(s32[]{:T(128)S(6)} %select_n.130, bf16[2,128,1536]{2,1,0:T(8,128)(2,1)} %bitcast.177, bf16[2,128,1536]{2,1,0:T(8,128)(2,1)} %bitcast.178, s32[]{:T(128)S(6)} %select_n.119, s32[]{:T(128)S(6)} %select_n.124, ...), kind=kLoop, calls=%fused_computation.51 | loop fusion | flops 6291456 | bytes 4718608 | tf_op jit(solution)/shard_map/jit(dynamic_index_in_dim)/squeeze | solution.py:48
  3.7 7.6 %collective-permute-start.5 = (bf16[128,3072]{1,0:T(8,128)(2,1)}, bf16[128,3072]{1,0:T(8,128)(2,1)}, u32[]{:S(2)}, u32[]{:S(2)}) collective-permute-start(bf16[128,3072]{1,0:T(8,128)(2,1)} %get-tuple-element.10), channel_id=1, source_target_pairs={{0,0},{1,8},{8,1},{9,9},{16,16},{17,24},{24,17},{25,25},{2,2},{3,1... | collective-permute-start | bytes 2359304 | tf_op jit(solution)/shard_map/ppermute | solution.py:49
  15.9 7.1 %collective-permute-start = (f32[16]{0:T(128)S(1)}, f32[16]{0:T(128)S(1)}, u32[]{:S(2)}, u32[]{:S(2)}) collective-permute-start(f32[16]{0:T(128)S(1)} %exp.32), channel_id=1, source_target_pairs={{0,8},{8,16},{16,24},{1,9},{9,17},{17,25},{2,10},{10,18},{18,26},{... | collective-permute-start | bytes 200 | tf_op jit(solution)/shard_map/ppermute | solution.py:18
  28.6 1.8 collective-permute-start.3
  30.4 6.1 %fusion.22 = f32[256,16,64]{0,2,1:T(8,128)} fusion(f32[256,16,64]{0,2,1:T(8,128)S(1)} %bitcast.170, f32[256,256]{1,0:T(8,128)S(1)} %fusion.54, f32[16,256]{1,0:T(8,128)S(1)} %copy-done.11, pred[256,256]{1,0:T(8,128)(4,1)S(1)} %iota_compare_fusion, f32[16]{0:T(128)S(1)} %copy-done.18), kind=kOutput, calls=%fused_computation.29 | convolution fusion | flops 810024960 | bytes 2441280 | tf_op jit(solution)/shard_map/hij,jhp->ihp/dot_general | solution.py:103
  37.3 7.3 %collective-permute-start.4 = (bf16[16,64,128]{2,1,0:T(8,128)(2,1)S(1)}, bf16[16,64,128]{2,1,0:T(8,128)(2,1)S(1)}, u32[]{:S(2)}, u32[]{:S(2)}) collective-permute-start(bf16[16,64,128]{2,1,0:T(8,128)(2,1)S(1)} %fusion.49), channel_id=1, source_target_pairs={{0,16},{8,24},{1,17},{9,25},{2,18},{10,26},{3,19},{11,27},{4,20},{... | collective-permute-start | bytes 786440 | tf_op jit(solution)/shard_map/ppermute | solution.py:18
  45.8 4.4 %collective-permute-start.1 = (f32[16]{0:T(128)S(1)}, f32[16]{0:T(128)S(1)}, u32[]{:S(2)}, u32[]{:S(2)}) collective-permute-start(f32[16]{0:T(128)S(1)} %collective-permute-done), channel_id=1, source_target_pairs={{0,8},{8,16},{16,24},{1,9},{9,17},{17,25},{2,10},{10,18},{18,26},{... | collective-permute-start | bytes 200 | tf_op jit(solution)/shard_map/ppermute | solution.py:18
  51.5 12.8 %collective-permute-start.17 = (bf16[192,1024]{1,0:T(8,128)(2,1)}, bf16[192,1024]{1,0:T(8,128)(2,1)}, u32[]{:S(2)}, u32[]{:S(2)}) collective-permute-start(bf16[192,1024]{1,0:T(8,128)(2,1)} %get-tuple-element.14), channel_id=1, source_target_pairs={{0,16},{1,24},{8,17},{9,25},{16,0},{17,8},{24,1},{25,9},{2,18},{3,... | collective-permute-start | bytes 1179656 | tf_op jit(solution)/shard_map/ppermute | solution.py:49
  66.6 3.0 %multiply_reduce_fusion.1 = (f32[256]{0:T(256)S(1)}, f32[256,16,64]{0,2,1:T(8,128)S(1)}) fusion(f32[256,16,64]{0,2,1:T(8,128)S(1)} %bitcast.176, f32[256,16,64]{0,2,1:T(8,128)} %fusion.22, f32[1,256,128]{2,1,0:T(8,128)S(1)} %copy-done, bf16[16,64,128]{2,1,0:T(8,128)(2,1)} %copy-done.17, bf16[16,64,128]{2,1,0:T(8,128)(2,1)S(1)} %collective-permute-done.2, ...), kind=kOutput, calls=%fused_computation.49 | convolution fusion | flops 405929728 | bytes 4080768 | tf_op jit(solution)/shard_map/in,hpn->ihp/dot_general | solution.py:105
  74.6 4.5 %scatter_custom_fusion = bf16[768,1024]{1,0:T(8,128)(2,1)} fusion(s32[512]{0:T(512)S(1)} %bitcast.179, bf16[512,1024]{1,0:T(8,128)(2,1)} %reshape.435, bf16[]{:T(256)} %constant.119.clone.1), kind=kCustom, calls=%fused_computation.66 | custom fusion | bytes 1573376 | tf_op jit(solution)/shard_map/scatter | solution.py:124
  79.1 5.2 %all-to-all-start = ((bf16[8,96,1024]{2,1,0:T(8,128)(2,1)}), bf16[8,96,1024]{2,1,0:T(8,128)(2,1)S(1)}, u32[]{:S(2)}, u32[]{:S(2)}) async-start(bf16[8,96,1024]{2,1,0:T(8,128)(2,1)} %bitcast.21), calls=%async_computation | async-start | bytes 3145728 | tf_op jit(solution)/shard_map/all_to_all | solution.py:125
  84.7 2.9 %collective-permute-start.11 = (bf16[128,3072]{1,0:T(8,128)(2,1)}, bf16[128,3072]{1,0:T(8,128)(2,1)S(1)}, u32[]{:S(2)}, u32[]{:S(2)}) collective-permute-start(bf16[128,3072]{1,0:T(8,128)(2,1)} %get-tuple-element.9), channel_id=1, source_target_pairs={{0,17},{1,25},{8,0},{9,8},{16,1},{17,9},{24,16},{25,24},{2,19},{3,... | collective-permute-start | bytes 2359304 | tf_op jit(solution)/shard_map/ppermute | solution.py:49
  95.3 26.4 %collective-permute-done.7 = bf16[128,3072]{1,0:T(8,128)(2,1)S(1)} collective-permute-done((bf16[128,3072]{1,0:T(8,128)(2,1)}, bf16[128,3072]{1,0:T(8,128)(2,1)S(1)}, u32[]{:S(2)}, u32[]{:S(2)}) %collective-permute-start.7) | collective-permute-done | bytes 786464 | tf_op jit(solution)/shard_map/ppermute | solution.py:49
  121.6 18.0 %collective-permute-done.9 = bf16[128,3072]{1,0:T(8,128)(2,1)S(1)} collective-permute-done((bf16[128,3072]{1,0:T(8,128)(2,1)}, bf16[128,3072]{1,0:T(8,128)(2,1)S(1)}, u32[]{:S(2)}, u32[]{:S(2)}) %collective-permute-start.9) | collective-permute-done | bytes 786464 | tf_op jit(solution)/shard_map/ppermute | solution.py:49
  139.7 16.6 %collective-permute-start.10 = (bf16[128,3072]{1,0:T(8,128)(2,1)S(1)}, bf16[128,3072]{1,0:T(8,128)(2,1)S(1)}, u32[]{:S(2)}, u32[]{:S(2)}) collective-permute-start(bf16[128,3072]{1,0:T(8,128)(2,1)S(1)} %collective-permute-done.9), channel_id=1, source_target_pairs={{0,1},{1,0},{2,3},{3,2},{4,5},{5,4},{6,7},{7,6},{8,9},{9,8},{10,11... | collective-permute-start | bytes 2359304 | tf_op jit(solution)/shard_map/ppermute | solution.py:50
  157.1 1.8 bitcast_dynamic-update-slice_fusion.9
  159.6 3.5 %broadcast_in_dim.103 = bf16[4,2,128,3072]{3,2,1,0:T(8,128)(2,1)} broadcast(bf16[]{:T(256)} %constant.119.clone.1), dimensions={} | broadcast | bytes 6291458 | tf_op jit(solution)/shard_map/broadcast_in_dim | solution.py:40
  163.1 2.1 bitcast_dynamic-update-slice_fusion.7
  171.9 7.3 %fusion.68 = f32[768,3072]{1,0:T(8,128)S(1)} fusion(bf16[768,1024]{1,0:T(8,128)(2,1)S(1)} %bitcast.174, bf16[1024,3072]{1,0:T(8,128)(2,1)} %bitcast.37), kind=kOutput, calls=%fused_computation.123 | convolution fusion | flops 4831838208 | bytes 17301504 | tf_op jit(solution)/shard_map/dot_general | solution.py:132
  179.2 4.0 %fusion.14 = bf16[768,1024]{1,0:T(8,128)(2,1)} fusion(bf16[1536,1024]{1,0:T(8,128)(2,1)S(1)} %bitcast.172, f32[768,3072]{1,0:T(8,128)S(1)} %fusion.68), kind=kOutput, calls=%fused_computation.24 | convolution fusion | flops 2423783424 | bytes 14155776 | tf_op jit(solution)/shard_map/dot_general | solution.py:136
  183.1 3.9 %all-to-all-start.1 = ((bf16[8,96,1024]{2,1,0:T(8,128)(2,1)}), bf16[8,96,1024]{2,1,0:T(8,128)(2,1)S(1)}, u32[]{:S(2)}, u32[]{:S(2)}) async-start(bf16[8,96,1024]{2,1,0:T(8,128)(2,1)} %bitcast.175), calls=%async_computation.1 | async-start | bytes 3145728 | tf_op jit(solution)/shard_map/all_to_all | solution.py:137
  188.4 19.5 %all-to-all-done.1 = bf16[8,96,1024]{2,1,0:T(8,128)(2,1)S(1)} async-done(((bf16[8,96,1024]{2,1,0:T(8,128)(2,1)}), bf16[8,96,1024]{2,1,0:T(8,128)(2,1)S(1)}, u32[]{:S(2)}, u32[]{:S(2)}) %all-to-all-start.1) | async-done | bytes 1572896 | tf_op jit(solution)/shard_map/all_to_all | solution.py:137
  208.0 2.8 %gather_fusion = bf16[512,1024]{1,0:T(8,128)(2,1)} fusion(bf16[768,1024]{1,0:T(8,128)(2,1)S(1)} %bitcast.167, s32[1024]{0:T(1024)S(1)} %pad_clamp_fusion), kind=kCustom, calls=%fused_computation | custom fusion | bytes 2099200 | tf_op jit(solution)/shard_map/gather | solution.py:144
  210.7 2.4 %reshape.422 = f32[256,2,1024]{2,1,0:T(2,128)S(1)} reshape(bf16[512,1024]{1,0:T(8,128)(2,1)} %gather_fusion) | data formatting | bytes 3145728 | tf_op jit(solution)/shard_map/convert_element_type | solution.py:144
  (127 shorter events, 41.3 us)
Async XLA Ops:
  0.0 28.2 %copy-start = (f32[1,256,128]{2,1,0:T(8,128)S(1)}, f32[1,256,128]{2,1,0:T(8,128)}, u32[]{:S(2)}) copy-start(f32[1,256,128]{2,1,0:T(8,128)} %param.17) | copy-start | bytes 393220
  3.7 91.0 %collective-permute-start.5 = (bf16[128,3072]{1,0:T(8,128)(2,1)}, bf16[128,3072]{1,0:T(8,128)(2,1)}, u32[]{:S(2)}, u32[]{:S(2)}) collective-permute-start(bf16[128,3072]{1,0:T(8,128)(2,1)} %get-tuple-element.10), channel_id=1, source_target_pairs={{0,0},{1,8},{8,1},{9,9},{16,16},{17,24},{24,17},{25,25},{2,2},{3,1... | collective-permute-start | bytes 2359304 | tf_op jit(solution)/shard_map/ppermute | solution.py:49
  14.5 14.0 %collective-permute-start.2 = (bf16[16,64,128]{2,1,0:T(8,128)(2,1)S(1)}, bf16[16,64,128]{2,1,0:T(8,128)(2,1)S(1)}, u32[]{:S(2)}, u32[]{:S(2)}) collective-permute-start(bf16[16,64,128]{2,1,0:T(8,128)(2,1)S(1)} %convolution_convert_fusion), channel_id=1, source_target_pairs={{0,8},{8,16},{16,24},{1,9},{9,17},{17,25},{2,10},{10,18},{18,26},{... | collective-permute-start | bytes 786440 | tf_op jit(solution)/shard_map/ppermute | solution.py:18
  15.9 20.9 %collective-permute-start = (f32[16]{0:T(128)S(1)}, f32[16]{0:T(128)S(1)}, u32[]{:S(2)}, u32[]{:S(2)}) collective-permute-start(f32[16]{0:T(128)S(1)} %exp.32), channel_id=1, source_target_pairs={{0,8},{8,16},{16,24},{1,9},{9,17},{17,25},{2,10},{10,18},{18,26},{... | collective-permute-start | bytes 200 | tf_op jit(solution)/shard_map/ppermute | solution.py:18
  24.1 40.2 %collective-permute-start.13 = (bf16[192,1024]{1,0:T(8,128)(2,1)S(1)}, bf16[192,1024]{1,0:T(8,128)(2,1)}, u32[]{:S(2)}, u32[]{:S(2)}) collective-permute-start(bf16[192,1024]{1,0:T(8,128)(2,1)S(1)} %get-tuple-element.16), channel_id=1, source_target_pairs={{0,0},{1,8},{8,1},{9,9},{16,16},{17,24},{24,17},{25,25},{2,2},{3,1... | collective-permute-start | bytes 1179656 | tf_op jit(solution)/shard_map/ppermute | solution.py:49
  25.5 58.8 %collective-permute-start.15 = (bf16[192,1024]{1,0:T(8,128)(2,1)}, bf16[192,1024]{1,0:T(8,128)(2,1)}, u32[]{:S(2)}, u32[]{:S(2)}) collective-permute-start(bf16[192,1024]{1,0:T(8,128)(2,1)} %get-tuple-element.15), channel_id=1, source_target_pairs={{0,1},{1,9},{8,16},{9,24},{16,17},{17,25},{24,0},{25,8},{2,3},{3,1... | collective-permute-start | bytes 1179656 | tf_op jit(solution)/shard_map/ppermute | solution.py:49
  28.6 8.6 %collective-permute-start.3 = (bf16[16,64,128]{2,1,0:T(8,128)(2,1)S(1)}, bf16[16,64,128]{2,1,0:T(8,128)(2,1)S(1)}, u32[]{:S(2)}, u32[]{:S(2)}) collective-permute-start(bf16[16,64,128]{2,1,0:T(8,128)(2,1)S(1)} %collective-permute-done.2), channel_id=1, source_target_pairs={{0,8},{8,16},{16,24},{1,9},{9,17},{17,25},{2,10},{10,18},{18,26},{... | collective-permute-start | bytes 786440 | tf_op jit(solution)/shard_map/ppermute | solution.py:18
  37.3 28.5 %collective-permute-start.4 = (bf16[16,64,128]{2,1,0:T(8,128)(2,1)S(1)}, bf16[16,64,128]{2,1,0:T(8,128)(2,1)S(1)}, u32[]{:S(2)}, u32[]{:S(2)}) collective-permute-start(bf16[16,64,128]{2,1,0:T(8,128)(2,1)S(1)} %fusion.49), channel_id=1, source_target_pairs={{0,16},{8,24},{1,17},{9,25},{2,18},{10,26},{3,19},{11,27},{4,20},{... | collective-permute-start | bytes 786440 | tf_op jit(solution)/shard_map/ppermute | solution.py:18
  45.8 5.7 %collective-permute-start.1 = (f32[16]{0:T(128)S(1)}, f32[16]{0:T(128)S(1)}, u32[]{:S(2)}, u32[]{:S(2)}) collective-permute-start(f32[16]{0:T(128)S(1)} %collective-permute-done), channel_id=1, source_target_pairs={{0,8},{8,16},{16,24},{1,9},{9,17},{17,25},{2,10},{10,18},{18,26},{... | collective-permute-start | bytes 200 | tf_op jit(solution)/shard_map/ppermute | solution.py:18
  51.5 32.9 %collective-permute-start.17 = (bf16[192,1024]{1,0:T(8,128)(2,1)}, bf16[192,1024]{1,0:T(8,128)(2,1)}, u32[]{:S(2)}, u32[]{:S(2)}) collective-permute-start(bf16[192,1024]{1,0:T(8,128)(2,1)} %get-tuple-element.14), channel_id=1, source_target_pairs={{0,16},{1,24},{8,17},{9,25},{16,0},{17,8},{24,1},{25,9},{2,18},{3,... | collective-permute-start | bytes 1179656 | tf_op jit(solution)/shard_map/ppermute | solution.py:49
  64.3 20.4 %collective-permute-start.19 = (bf16[192,1024]{1,0:T(8,128)(2,1)}, bf16[192,1024]{1,0:T(8,128)(2,1)}, u32[]{:S(2)}, u32[]{:S(2)}) collective-permute-start(bf16[192,1024]{1,0:T(8,128)(2,1)} %get-tuple-element.13), channel_id=1, source_target_pairs={{0,17},{1,25},{8,0},{9,8},{16,1},{17,9},{24,16},{25,24},{2,19},{3,... | collective-permute-start | bytes 1179656 | tf_op jit(solution)/shard_map/ppermute | solution.py:49
  65.8 21.8 %collective-permute-start.14 = (bf16[192,1024]{1,0:T(8,128)(2,1)}, bf16[192,1024]{1,0:T(8,128)(2,1)}, u32[]{:S(2)}, u32[]{:S(2)}) collective-permute-start(bf16[192,1024]{1,0:T(8,128)(2,1)} %collective-permute-done.13), channel_id=1, source_target_pairs={{0,1},{1,0},{2,3},{3,2},{4,5},{5,4},{6,7},{7,6},{8,9},{9,8},{10,11... | collective-permute-start | bytes 1179656 | tf_op jit(solution)/shard_map/ppermute | solution.py:50
  79.1 92.8 %all-to-all-start = ((bf16[8,96,1024]{2,1,0:T(8,128)(2,1)}), bf16[8,96,1024]{2,1,0:T(8,128)(2,1)S(1)}, u32[]{:S(2)}, u32[]{:S(2)}) async-start(bf16[8,96,1024]{2,1,0:T(8,128)(2,1)} %bitcast.21), calls=%async_computation | async-start | bytes 3145728 | tf_op jit(solution)/shard_map/all_to_all | solution.py:125
  84.3 37.3 %collective-permute-start.7 = (bf16[128,3072]{1,0:T(8,128)(2,1)}, bf16[128,3072]{1,0:T(8,128)(2,1)S(1)}, u32[]{:S(2)}, u32[]{:S(2)}) collective-permute-start(bf16[128,3072]{1,0:T(8,128)(2,1)} %get-tuple-element.11), channel_id=1, source_target_pairs={{0,1},{1,9},{8,16},{9,24},{16,17},{17,25},{24,0},{25,8},{2,3},{3,1... | collective-permute-start | bytes 2359304 | tf_op jit(solution)/shard_map/ppermute | solution.py:49
  84.4 55.3 %collective-permute-start.9 = (bf16[128,3072]{1,0:T(8,128)(2,1)}, bf16[128,3072]{1,0:T(8,128)(2,1)S(1)}, u32[]{:S(2)}, u32[]{:S(2)}) collective-permute-start(bf16[128,3072]{1,0:T(8,128)(2,1)} %get-tuple-element.12), channel_id=1, source_target_pairs={{0,16},{1,24},{8,17},{9,25},{16,0},{17,8},{24,1},{25,9},{2,18},{3,... | collective-permute-start | bytes 2359304 | tf_op jit(solution)/shard_map/ppermute | solution.py:49
  84.7 55.0 %collective-permute-start.11 = (bf16[128,3072]{1,0:T(8,128)(2,1)}, bf16[128,3072]{1,0:T(8,128)(2,1)S(1)}, u32[]{:S(2)}, u32[]{:S(2)}) collective-permute-start(bf16[128,3072]{1,0:T(8,128)(2,1)} %get-tuple-element.9), channel_id=1, source_target_pairs={{0,17},{1,25},{8,0},{9,8},{16,1},{17,9},{24,16},{25,24},{2,19},{3,... | collective-permute-start | bytes 2359304 | tf_op jit(solution)/shard_map/ppermute | solution.py:49
  87.6 4.6 %collective-permute-start.16 = (bf16[192,1024]{1,0:T(8,128)(2,1)}, bf16[192,1024]{1,0:T(8,128)(2,1)S(1)}, u32[]{:S(2)}, u32[]{:S(2)}) collective-permute-start(bf16[192,1024]{1,0:T(8,128)(2,1)} %collective-permute-done.15), channel_id=1, source_target_pairs={{0,1},{1,0},{2,3},{3,2},{4,5},{5,4},{6,7},{7,6},{8,9},{9,8},{10,11... | collective-permute-start | bytes 1179656 | tf_op jit(solution)/shard_map/ppermute | solution.py:50
  92.2 64.1 %collective-permute-start.18 = (bf16[192,1024]{1,0:T(8,128)(2,1)}, bf16[192,1024]{1,0:T(8,128)(2,1)S(1)}, u32[]{:S(2)}, u32[]{:S(2)}) collective-permute-start(bf16[192,1024]{1,0:T(8,128)(2,1)} %collective-permute-done.17), channel_id=1, source_target_pairs={{0,1},{1,0},{2,3},{3,2},{4,5},{5,4},{6,7},{7,6},{8,9},{9,8},{10,11... | collective-permute-start | bytes 1179656 | tf_op jit(solution)/shard_map/ppermute | solution.py:50
  94.7 64.1 %collective-permute-start.20 = (bf16[192,1024]{1,0:T(8,128)(2,1)}, bf16[192,1024]{1,0:T(8,128)(2,1)S(1)}, u32[]{:S(2)}, u32[]{:S(2)}) collective-permute-start(bf16[192,1024]{1,0:T(8,128)(2,1)} %collective-permute-done.19), channel_id=1, source_target_pairs={{0,1},{1,0},{2,3},{3,2},{4,5},{5,4},{6,7},{7,6},{8,9},{9,8},{10,11... | collective-permute-start | bytes 1179656 | tf_op jit(solution)/shard_map/ppermute | solution.py:50
  121.6 43.5 %collective-permute-start.6 = (bf16[128,3072]{1,0:T(8,128)(2,1)}, bf16[128,3072]{1,0:T(8,128)(2,1)S(1)}, u32[]{:S(2)}, u32[]{:S(2)}) collective-permute-start(bf16[128,3072]{1,0:T(8,128)(2,1)} %collective-permute-done.5), channel_id=1, source_target_pairs={{0,1},{1,0},{2,3},{3,2},{4,5},{5,4},{6,7},{7,6},{8,9},{9,8},{10,11... | collective-permute-start | bytes 2359304 | tf_op jit(solution)/shard_map/ppermute | solution.py:50
  139.7 27.4 %collective-permute-start.8 = (bf16[128,3072]{1,0:T(8,128)(2,1)S(1)}, bf16[128,3072]{1,0:T(8,128)(2,1)S(1)}, u32[]{:S(2)}, u32[]{:S(2)}) collective-permute-start(bf16[128,3072]{1,0:T(8,128)(2,1)S(1)} %collective-permute-done.7), channel_id=1, source_target_pairs={{0,1},{1,0},{2,3},{3,2},{4,5},{5,4},{6,7},{7,6},{8,9},{9,8},{10,11... | collective-permute-start | bytes 2359304 | tf_op jit(solution)/shard_map/ppermute | solution.py:50
  139.7 29.4 %collective-permute-start.10 = (bf16[128,3072]{1,0:T(8,128)(2,1)S(1)}, bf16[128,3072]{1,0:T(8,128)(2,1)S(1)}, u32[]{:S(2)}, u32[]{:S(2)}) collective-permute-start(bf16[128,3072]{1,0:T(8,128)(2,1)S(1)} %collective-permute-done.9), channel_id=1, source_target_pairs={{0,1},{1,0},{2,3},{3,2},{4,5},{5,4},{6,7},{7,6},{8,9},{9,8},{10,11... | collective-permute-start | bytes 2359304 | tf_op jit(solution)/shard_map/ppermute | solution.py:50
  156.3 14.7 %collective-permute-start.12 = (bf16[128,3072]{1,0:T(8,128)(2,1)S(1)}, bf16[128,3072]{1,0:T(8,128)(2,1)S(1)}, u32[]{:S(2)}, u32[]{:S(2)}) collective-permute-start(bf16[128,3072]{1,0:T(8,128)(2,1)S(1)} %collective-permute-done.11), channel_id=1, source_target_pairs={{0,1},{1,0},{2,3},{3,2},{4,5},{5,4},{6,7},{7,6},{8,9},{9,8},{10,11... | collective-permute-start | bytes 2359304 | tf_op jit(solution)/shard_map/ppermute | solution.py:50
  183.1 24.8 %all-to-all-start.1 = ((bf16[8,96,1024]{2,1,0:T(8,128)(2,1)}), bf16[8,96,1024]{2,1,0:T(8,128)(2,1)S(1)}, u32[]{:S(2)}, u32[]{:S(2)}) async-start(bf16[8,96,1024]{2,1,0:T(8,128)(2,1)} %bitcast.175), calls=%async_computation.1 | async-start | bytes 3145728 | tf_op jit(solution)/shard_map/all_to_all | solution.py:137
  (18 other events, 161.4 us)

commit v2 on v1

--- a/solution.py
+++ b/solution.py
@@ -11,33 +11,19 @@
 
 
 def state_before(through, local_end):
-    count = lax.axis_size(TM)
-
-    def shifted(value, by):
-        pairs = [(z, z + by) for z in range(count - by)]
-        return lax.ppermute(value, TM, pairs)
-
-    decay = shifted(through, 1)
-    state = shifted(local_end.astype(jnp.bfloat16), 1).astype(jnp.float32)
-    by = 1
-    while by < count - 1:
-        earlier = shifted(state.astype(jnp.bfloat16), by).astype(jnp.float32)
-        state = decay[:, None, None] * earlier + state
-        if 2 * by < count - 1:
-            decay = decay * shifted(decay, by)
-        by *= 2
+    state = jnp.zeros_like(local_end)
+    for place in range(lax.axis_size(TM) - 1):
+        end = through[:, None, None] * state + local_end
+        came = lax.ppermute(end.astype(jnp.bfloat16), TM, [(place, place + 1)])
+        state = state + came.astype(jnp.float32)
     return state
 
 
-def whole_expert(shard, exchange_axes):
+def sent_rows(shard, after):
     count = lax.axis_size(TM)
     place = lax.axis_index(TM)
-    core = lax.axis_index("core")
-    group = lax.axis_index("zh")
-    rows, width = shard.shape
-    half = rows // 2
-    halves = shard.reshape(2, half, width)
-    full = jnp.zeros((count, 2, half, width), shard.dtype)
+    half = shard.shape[0] // 2
+    arrived = []
     for turn in range(count):
         pairs = []
         for z in range(count):
@@ -45,14 +31,25 @@
             for owned in range(2):
                 pairs.append((z * 2 + owned, (owned + 2 * (spot // 2)) * 2 + spot % 2))
         wanted = lax.rem(place + turn, 2)
-        piece = lax.dynamic_index_in_dim(halves, wanted, 0, keepdims=False)
-        mine = lax.ppermute(piece, exchange_axes, pairs)
-        other = lax.ppermute(mine, "core", [(0, 1), (1, 0)])
-        origin = lax.rem(2 * group + core - turn + count, count)
-        origin_other = lax.rem(2 * group + 1 - core - turn + count, count)
-        full = lax.dynamic_update_slice(full, mine[None, None], (origin, core, 0, 0))
-        full = lax.dynamic_update_slice(full, other[None, None], (origin_other, 1 - core, 0, 0))
-    return full.reshape(count * rows, width)
+        piece = lax.dynamic_slice(shard, (wanted * half, 0), (half, shard.shape[1]))
+        if after is not None:
+            piece, _ = lax.optimization_barrier((piece, after[turn]))
+        arrived.append(lax.ppermute(piece, ("zh", "zp", "core"), pairs))
+    return arrived
+
+
+def joined_rows(arrived):
+    count = lax.axis_size(TM)
+    core = lax.axis_index("core")
+    group = lax.axis_index("zh")
+    half, width = arrived[0].shape
+    full = jnp.zeros((count, 2, half, width), arrived[0].dtype)
+    for turn in range(count):
+        other = lax.ppermute(arrived[turn], "core", [(0, 1), (1, 0)])
+        for piece, side in ((arrived[turn], core), (other, 1 - core)):
+            origin = lax.rem(2 * group + side - turn + count, count)
+            full = lax.dynamic_update_slice(full, piece[None, None], (origin, side, 0, 0))
+    return full.reshape(count * 2 * half, width)
 
 
 def rms_scale(rows, gain):
@@ -81,8 +78,10 @@
     length = x_in.shape[1]
     hidden_width = w_gate.shape[2]
 
-    both = whole_expert(jnp.concatenate([w_gate[0], w_up[0]], axis=1), ("zh", "zp", "core"))
-    down = whole_expert(w_down[0], ("zh", "zp", "core"))
+    wide_pieces = sent_rows(jnp.concatenate([w_gate[0], w_up[0]], axis=1), None)
+    down_pieces = sent_rows(w_down[0], wide_pieces)
+    both = joined_rows(wide_pieces)
+    down = joined_rows(down_pieces)
 
     values = x_in[0].reshape(length, heads, width)
     b_rows = b_proj[0]

time: 218 us -> 210 us (0.963)
  waiting for transfers between devices: 65.7 us -> 53.5 us
  local copies, waits for them, and re-layouts: 43 us -> 45.5 us
    all_to_all x1, starting transfers between devices: 5.18 us -> 27.9 us  [per_device(): lax.all_to_all(outgoing.reshape(expert_count, capacity, model_width), ('z...]
    ppermute x21 -> x19, starting transfers between devices: 66.1 us -> 43.9 us  [the longest x8 24.8 us: sent_rows(): arrived.append(lax.ppermute(piece, ('zh', 'zp', 'core'), pairs))]
    ppermute x21 -> x19, waiting for transfers between devices: 46.2 us -> 34 us  [the longest x3 29.3 us: state_before(): came = lax.ppermute(end.astype(jnp.bfloat16), TM, [(place, place + 1)])]
    squeeze x1 -> x0, other arithmetic: 3.71 us -> none  [whole_expert(): piece = lax.dynamic_index_in_dim(halves, wanted, 0, keepdims=False)]
    concatenate x0 -> x1, other arithmetic: none -> 3.58 us  [per_device(): wide_pieces = sent_rows(jnp.concatenate([w_gate[0], w_up[0]], axis=1), None)]
  transfers between devices with their start and end apart: 23 -> 21, of which waited for: 5 -> 3; matrix products, arithmetic and copies ran while one was open for 24% -> 25% of each run, Pallas kernels for 0% -> 0%
where the time goes in v2:
time: 210 us; the launch traced here: 208 us
  starting transfers between devices  75.8 us (36%)
  waiting for transfers between devices  53.5 us (25%)
  local copies, waits for them, and re-layouts  45.5 us (22%)
  matrix products  23.4 us (11%)
  other arithmetic  9.63 us (5%)
    ppermute x3, waiting for transfers between devices, state_before(): came = lax.ppermute(end.astype(jnp.bfloat16), TM, [(place, place + 1)])  29.3 us
    all_to_all x1, starting transfers between devices, per_device(): lax.all_to_all(outgoing.reshape(expert_count, capacity, model_width), ('z...  27.9 us
    ppermute x8, starting transfers between devices, sent_rows(): arrived.append(lax.ppermute(piece, ('zh', 'zp', 'core'), pairs))  24.8 us
    all_to_all x1, waiting for transfers between devices, per_device(): lax.all_to_all(produced.reshape(expert_count, capacity, model_width), ('z...  19.6 us
    dynamic_update_slice x16, local copies, waits for them, and re-layouts, joined_rows(): lax.dynamic_update_slice(full, piece[None, None], (origin, side, 0, 0))  18.4 us
    ppermute x8, starting transfers between devices, joined_rows(): other = lax.ppermute(arrived[turn], 'core', [(0, 1), (1, 0)])  15.5 us
    dot_general x1, matrix products, per_device(): gate_up = jnp.dot(received, both, preferred_element_type=jnp.float32)  7.11 us
    dot_general x1, matrix products, per_device(): jnp.einsum('hij,jhp->ihp', masked * scores[None], values, precision=exact...  6.13 us
  transfers between devices with their start and end apart: 21, of which 3 were waited for; matrix products, arithmetic and copies ran while one was open for 25% of the time, Pallas kernels for 0%

profile of v2, /device:TPU:0, one launch (start us, length us, event | category | flops | bytes accessed | tf_op | source)
XLA Modules:
  0.0 208.3 jit_solution(11036725222706004783)
XLA Ops:
  0.0 3.6 %fusion.36 = (bf16[128,3072]{1,0:T(8,128)(2,1)}, bf16[128,3072]{1,0:T(8,128)(2,1)}, bf16[128,3072]{1,0:T(8,128)(2,1)}, bf16[128,3072]{1,0:T(8,128)(2,1)}) fusion(s32[]{:T(128)S(6)} %select_n.136, bf16[256,1536]{1,0:T(8,128)(2,1)} %bitcast.168, bf16[256,1536]{1,0:T(8,128)(2,1)} %bitcast.169, s32[]{:T(128)S(6)} %select_n.125, s32[]{:T(128)S(6)} %select_n.130, ...), kind=kLoop, calls=%fused_computation.49 | loop fusion | flops 6291456 | bytes 4718608 | tf_op jit(solution)/shard_map/concatenate | solution.py:81
  3.6 7.5 %collective-permute-start.3 = (bf16[128,3072]{1,0:T(8,128)(2,1)}, bf16[128,3072]{1,0:T(8,128)(2,1)}, u32[]{:S(2)}, u32[]{:S(2)}) collective-permute-start(bf16[128,3072]{1,0:T(8,128)(2,1)} %get-tuple-element.18), channel_id=1, source_target_pairs={{0,0},{1,8},{8,1},{9,9},{16,16},{17,24},{24,17},{25,25},{2,2},{3,1... | collective-permute-start | bytes 2359304 | tf_op jit(solution)/shard_map/ppermute | solution.py:37
  11.1 4.0 %collective-permute-start.7 = (bf16[128,3072]{1,0:T(8,128)(2,1)}, bf16[128,3072]{1,0:T(8,128)(2,1)}, u32[]{:S(2)}, u32[]{:S(2)}) collective-permute-start(bf16[128,3072]{1,0:T(8,128)(2,1)} %get-tuple-element.20), channel_id=1, source_target_pairs={{0,16},{1,24},{8,17},{9,25},{16,0},{17,8},{24,1},{25,9},{2,18},{3,... | collective-permute-start | bytes 2359304 | tf_op jit(solution)/shard_map/ppermute | solution.py:37
  20.8 2.2 %collective-permute-start = (bf16[16,64,128]{2,1,0:T(8,128)(2,1)S(1)}, bf16[16,64,128]{2,1,0:T(8,128)(2,1)S(1)}, u32[]{:S(2)}, u32[]{:S(2)}) collective-permute-start(bf16[16,64,128]{2,1,0:T(8,128)(2,1)S(1)} %get-tuple-element.33), channel_id=1, source_target_pairs={{0,8},{1,9},{2,10},{3,11},{4,12},{5,13},{6,14},{7,15}} | collective-permute-start | bytes 786440 | tf_op jit(solution)/shard_map/ppermute | solution.py:17
  26.5 29.3 %collective-permute-done = bf16[16,64,128]{2,1,0:T(8,128)(2,1)S(1)} collective-permute-done((bf16[16,64,128]{2,1,0:T(8,128)(2,1)S(1)}, bf16[16,64,128]{2,1,0:T(8,128)(2,1)S(1)}, u32[]{:S(2)}, u32[]{:S(2)}) %collective-permute-start) | collective-permute-done | bytes 262176 | tf_op jit(solution)/shard_map/ppermute | solution.py:17
  56.7 6.1 %fusion.22 = f32[256,16,64]{0,2,1:T(8,128)} fusion(f32[256,16,64]{0,2,1:T(8,128)S(1)} %bitcast.163, f32[256,256]{1,0:T(8,128)S(1)} %fusion.49, f32[16,256]{1,0:T(8,128)S(1)} %get-tuple-element.28, pred[256,256]{1,0:T(8,128)(4,1)S(1)} %iota_compare_fusion, f32[16]{0:T(128)S(1)} %copy-done.13), kind=kOutput, calls=%fused_computation.29 | convolution fusion | flops 810024960 | bytes 2441280 | tf_op jit(solution)/shard_map/hij,jhp->ihp/dot_general | solution.py:102
  65.9 2.9 %multiply_reduce_fusion.1 = (f32[256]{0:T(256)S(1)}, f32[256,16,64]{0,2,1:T(8,128)S(1)}) fusion(f32[256,16,64]{0,2,1:T(8,128)} %bitcast.167, f32[256,16,64]{0,2,1:T(8,128)} %fusion.22, f32[1,256,128]{2,1,0:T(8,128)S(1)} %copy-done, bf16[16,64,128]{2,1,0:T(8,128)(2,1)} %copy-done.12, bf16[16,64,128]{2,1,0:T(8,128)(2,1)S(1)} %collective-permute-done.1, ...), kind=kOutput, calls=%fused_computation.48 | convolution fusion | flops 405667584 | bytes 4080640 | tf_op jit(solution)/shard_map/in,hpn->ihp/dot_general | solution.py:104
  73.8 4.5 %scatter_custom_fusion = bf16[768,1024]{1,0:T(8,128)(2,1)} fusion(s32[512]{0:T(512)S(1)} %bitcast.170, bf16[512,1024]{1,0:T(8,128)(2,1)} %reshape.437, bf16[]{:T(256)} %constant.108.clone.1), kind=kCustom, calls=%fused_computation.61 | custom fusion | bytes 1573376 | tf_op jit(solution)/shard_map/scatter | solution.py:123
  78.3 27.9 %all-to-all-start = ((bf16[8,96,1024]{2,1,0:T(8,128)(2,1)}), bf16[8,96,1024]{2,1,0:T(8,128)(2,1)S(1)}, u32[]{:S(2)}, u32[]{:S(2)}) async-start(bf16[8,96,1024]{2,1,0:T(8,128)(2,1)} %bitcast.21), calls=%async_computation | async-start | bytes 3145728 | tf_op jit(solution)/shard_map/all_to_all | solution.py:124
  107.9 2.5 %collective-permute-start.13 = (bf16[192,1024]{1,0:T(8,128)(2,1)}, bf16[192,1024]{1,0:T(8,128)(2,1)S(1)}, u32[]{:S(2)}, u32[]{:S(2)}) collective-permute-start(bf16[192,1024]{1,0:T(8,128)(2,1)} %get-tuple-element.10), channel_id=1, source_target_pairs={{0,1},{1,9},{8,16},{9,24},{16,17},{17,25},{24,0},{25,8},{2,3},{3,1... | collective-permute-start | bytes 1179656 | tf_op jit(solution)/shard_map/ppermute | solution.py:37
  110.4 7.4 %collective-permute-start.15 = (bf16[192,1024]{1,0:T(8,128)(2,1)}, bf16[192,1024]{1,0:T(8,128)(2,1)S(1)}, u32[]{:S(2)}, u32[]{:S(2)}) collective-permute-start(bf16[192,1024]{1,0:T(8,128)(2,1)} %get-tuple-element.11), channel_id=1, source_target_pairs={{0,16},{1,24},{8,17},{9,25},{16,0},{17,8},{24,1},{25,9},{2,18},{3,... | collective-permute-start | bytes 1179656 | tf_op jit(solution)/shard_map/ppermute | solution.py:37
  119.6 3.4 %broadcast_in_dim.108 = bf16[4,2,128,3072]{3,2,1,0:T(8,128)(2,1)} broadcast(bf16[]{:T(256)} %constant.108.clone.1), dimensions={} | broadcast | bytes 6291458 | tf_op jit(solution)/shard_map/broadcast_in_dim | solution.py:46
  123.1 2.1 %bitcast_dynamic-update-slice_fusion.7 = bf16[4,2,128,3072]{3,2,1,0:T(8,128)(2,1)} fusion(bf16[4,2,128,3072]{3,2,1,0:T(8,128)(2,1)} %broadcast_in_dim.108, s32[]{:T(128)S(6)} %select_n.126, s32[]{:T(128)S(6)} %select_n.127, bf16[128,3072]{1,0:T(8,128)(2,1)} %collective-permute-done.3), kind=kLoop, calls=%fused_computation.60 | loop fusion | bytes 1572872 | tf_op jit(solution)/shard_map/dynamic_update_slice | solution.py:51
  125.1 7.1 %collective-permute-start.6 = (bf16[128,3072]{1,0:T(8,128)(2,1)}, bf16[128,3072]{1,0:T(8,128)(2,1)S(1)}, u32[]{:S(2)}, u32[]{:S(2)}) collective-permute-start(bf16[128,3072]{1,0:T(8,128)(2,1)} %collective-permute-done.5), channel_id=1, source_target_pairs={{0,1},{1,0},{2,3},{3,2},{4,5},{5,4},{6,7},{7,6},{8,9},{9,8},{10,11... | collective-permute-start | bytes 2359304 | tf_op jit(solution)/shard_map/ppermute | solution.py:48
  132.2 2.1 %broadcast_in_dim.117 = bf16[4,2,192,1024]{3,2,1,0:T(8,128)(2,1)} broadcast(bf16[]{:T(256)} %constant.108.clone.1), dimensions={} | broadcast | bytes 3145730 | tf_op jit(solution)/shard_map/broadcast_in_dim | solution.py:46
  136.1 2.1 %bitcast_dynamic-update-slice_fusion.5 = bf16[4,2,128,3072]{3,2,1,0:T(8,128)(2,1)} fusion(bf16[4,2,128,3072]{3,2,1,0:T(8,128)(2,1)} %bitcast_dynamic-update-slice_fusion.6, s32[]{:T(128)S(6)} %select_n.131, s32[]{:T(128)S(6)} %select_n.127, bf16[128,3072]{1,0:T(8,128)(2,1)} %collective-permute-done.5), kind=kLoop, calls=%fused_computation.58 | loop fusion | bytes 1572872 | tf_op jit(solution)/shard_map/dynamic_update_slice | solution.py:51
  141.8 4.6 %collective-permute-done.13 = bf16[192,1024]{1,0:T(8,128)(2,1)S(1)} collective-permute-done((bf16[192,1024]{1,0:T(8,128)(2,1)}, bf16[192,1024]{1,0:T(8,128)(2,1)S(1)}, u32[]{:S(2)}, u32[]{:S(2)}) %collective-permute-start.13) | collective-permute-done | bytes 393248 | tf_op jit(solution)/shard_map/ppermute | solution.py:37
  146.4 4.0 %collective-permute-start.14 = (bf16[192,1024]{1,0:T(8,128)(2,1)S(1)}, bf16[192,1024]{1,0:T(8,128)(2,1)S(1)}, u32[]{:S(2)}, u32[]{:S(2)}) collective-permute-start(bf16[192,1024]{1,0:T(8,128)(2,1)S(1)} %collective-permute-done.13), channel_id=1, source_target_pairs={{0,1},{1,0},{2,3},{3,2},{4,5},{5,4},{6,7},{7,6},{8,9},{9,8},{10,11... | collective-permute-start | bytes 1179656 | tf_op jit(solution)/shard_map/ppermute | solution.py:48
  162.0 7.1 %fusion.64 = f32[768,3072]{1,0:T(8,128)S(1)} fusion(bf16[768,1024]{1,0:T(8,128)(2,1)S(1)} %bitcast.165, bf16[1024,3072]{1,0:T(8,128)(2,1)} %bitcast.33), kind=kOutput, calls=%fused_computation.122 | convolution fusion | flops 4831838208 | bytes 17301504 | tf_op jit(solution)/shard_map/dot_general | solution.py:131
  169.1 5.9 %fusion.14 = bf16[768,1024]{1,0:T(8,128)(2,1)} fusion(bf16[1536,1024]{1,0:T(8,128)(2,1)} %bitcast.46, f32[768,3072]{1,0:T(8,128)S(1)} %fusion.64), kind=kOutput, calls=%fused_computation.24 | convolution fusion | flops 2423783424 | bytes 14155776 | tf_op jit(solution)/shard_map/dot_general | solution.py:135
  175.0 3.9 %all-to-all-start.1 = ((bf16[8,96,1024]{2,1,0:T(8,128)(2,1)}), bf16[8,96,1024]{2,1,0:T(8,128)(2,1)S(1)}, u32[]{:S(2)}, u32[]{:S(2)}) async-start(bf16[8,96,1024]{2,1,0:T(8,128)(2,1)} %bitcast.166), calls=%async_computation.1 | async-start | bytes 3145728 | tf_op jit(solution)/shard_map/all_to_all | solution.py:136
  180.2 19.6 %all-to-all-done.1 = bf16[8,96,1024]{2,1,0:T(8,128)(2,1)S(1)} async-done(((bf16[8,96,1024]{2,1,0:T(8,128)(2,1)}), bf16[8,96,1024]{2,1,0:T(8,128)(2,1)S(1)}, u32[]{:S(2)}, u32[]{:S(2)}) %all-to-all-start.1) | async-done | bytes 1572896 | tf_op jit(solution)/shard_map/all_to_all | solution.py:136
  199.8 2.8 %gather_fusion = bf16[512,1024]{1,0:T(8,128)(2,1)} fusion(bf16[768,1024]{1,0:T(8,128)(2,1)S(1)} %bitcast.160, s32[1024]{0:T(1024)S(1)} %pad_clamp_fusion), kind=kCustom, calls=%fused_computation | custom fusion | bytes 2099200 | tf_op jit(solution)/shard_map/gather | solution.py:143
  202.6 2.4 %reshape.424 = f32[256,2,1024]{2,1,0:T(2,128)S(1)} reshape(bf16[512,1024]{1,0:T(8,128)(2,1)} %gather_fusion) | data formatting | bytes 3145728 | tf_op jit(solution)/shard_map/convert_element_type | solution.py:143
  (113 shorter events, 42.8 us)
Async XLA Ops:
  0.0 26.2 %copy-start = (f32[1,256,128]{2,1,0:T(8,128)S(1)}, f32[1,256,128]{2,1,0:T(8,128)}, u32[]{:S(2)}) copy-start(f32[1,256,128]{2,1,0:T(8,128)} %param.17) | copy-start | bytes 393220
  0.0 16.9 %copy-start.7 = (f32[1,256,16]{1,2,0:T(8,128)S(1)}, f32[1,256,16]{1,2,0:T(8,128)}, u32[]{:S(2)}) copy-start(f32[1,256,16]{1,2,0:T(8,128)} %param.18) | copy-start | bytes 49156
  3.6 102.7 %collective-permute-start.3 = (bf16[128,3072]{1,0:T(8,128)(2,1)}, bf16[128,3072]{1,0:T(8,128)(2,1)}, u32[]{:S(2)}, u32[]{:S(2)}) collective-permute-start(bf16[128,3072]{1,0:T(8,128)(2,1)} %get-tuple-element.18), channel_id=1, source_target_pairs={{0,0},{1,8},{8,1},{9,9},{16,16},{17,24},{24,17},{25,25},{2,2},{3,1... | collective-permute-start | bytes 2359304 | tf_op jit(solution)/shard_map/ppermute | solution.py:37
  11.1 96.8 %collective-permute-start.5 = (bf16[128,3072]{1,0:T(8,128)(2,1)}, bf16[128,3072]{1,0:T(8,128)(2,1)}, u32[]{:S(2)}, u32[]{:S(2)}) collective-permute-start(bf16[128,3072]{1,0:T(8,128)(2,1)} %get-tuple-element.19), channel_id=1, source_target_pairs={{0,1},{1,9},{8,16},{9,24},{16,17},{17,25},{24,0},{25,8},{2,3},{3,1... | collective-permute-start | bytes 2359304 | tf_op jit(solution)/shard_map/ppermute | solution.py:37
  11.1 99.3 %collective-permute-start.7 = (bf16[128,3072]{1,0:T(8,128)(2,1)}, bf16[128,3072]{1,0:T(8,128)(2,1)}, u32[]{:S(2)}, u32[]{:S(2)}) collective-permute-start(bf16[128,3072]{1,0:T(8,128)(2,1)} %get-tuple-element.20), channel_id=1, source_target_pairs={{0,16},{1,24},{8,17},{9,25},{16,0},{17,8},{24,1},{25,9},{2,18},{3,... | collective-permute-start | bytes 2359304 | tf_op jit(solution)/shard_map/ppermute | solution.py:37
  15.2 102.6 %collective-permute-start.9 = (bf16[128,3072]{1,0:T(8,128)(2,1)}, bf16[128,3072]{1,0:T(8,128)(2,1)}, u32[]{:S(2)}, u32[]{:S(2)}) collective-permute-start(bf16[128,3072]{1,0:T(8,128)(2,1)} %get-tuple-element.17), channel_id=1, source_target_pairs={{0,17},{1,25},{8,0},{9,8},{16,1},{17,9},{24,16},{25,24},{2,19},{3,... | collective-permute-start | bytes 2359304 | tf_op jit(solution)/shard_map/ppermute | solution.py:37
  19.8 36.9 %copy-start.13 = (f32[16]{0:T(128)S(1)}, f32[16]{0:T(128)}, u32[]{:S(2)}) copy-start(f32[16]{0:T(128)} %param.19) | copy-start | bytes 196
  20.8 35.1 %collective-permute-start = (bf16[16,64,128]{2,1,0:T(8,128)(2,1)S(1)}, bf16[16,64,128]{2,1,0:T(8,128)(2,1)S(1)}, u32[]{:S(2)}, u32[]{:S(2)}) collective-permute-start(bf16[16,64,128]{2,1,0:T(8,128)(2,1)S(1)} %get-tuple-element.33), channel_id=1, source_target_pairs={{0,8},{1,9},{2,10},{3,11},{4,12},{5,13},{6,14},{7,15}} | collective-permute-start | bytes 786440 | tf_op jit(solution)/shard_map/ppermute | solution.py:17
  56.0 6.8 %collective-permute-start.1 = (bf16[16,64,128]{2,1,0:T(8,128)(2,1)S(1)}, bf16[16,64,128]{2,1,0:T(8,128)(2,1)S(1)}, u32[]{:S(2)}, u32[]{:S(2)}) collective-permute-start(bf16[16,64,128]{2,1,0:T(8,128)(2,1)S(1)} %fusion.43), channel_id=1, source_target_pairs={{8,16},{9,17},{10,18},{11,19},{12,20},{13,21},{14,22},{15,23}} | collective-permute-start | bytes 786440 | tf_op jit(solution)/shard_map/ppermute | solution.py:17
  63.0 2.2 %collective-permute-start.2 = (bf16[16,64,128]{2,1,0:T(8,128)(2,1)S(1)}, bf16[16,64,128]{2,1,0:T(8,128)(2,1)S(1)}, u32[]{:S(2)}, u32[]{:S(2)}) collective-permute-start(bf16[16,64,128]{2,1,0:T(8,128)(2,1)S(1)} %add_convert_fusion), channel_id=1, source_target_pairs={{16,24},{17,25},{18,26},{19,27},{20,28},{21,29},{22,30},{23,31}} | collective-permute-start | bytes 786440 | tf_op jit(solution)/shard_map/ppermute | solution.py:17
  78.3 83.6 %all-to-all-start = ((bf16[8,96,1024]{2,1,0:T(8,128)(2,1)}), bf16[8,96,1024]{2,1,0:T(8,128)(2,1)S(1)}, u32[]{:S(2)}, u32[]{:S(2)}) async-start(bf16[8,96,1024]{2,1,0:T(8,128)(2,1)} %bitcast.21), calls=%async_computation | async-start | bytes 3145728 | tf_op jit(solution)/shard_map/all_to_all | solution.py:124
  106.3 18.9 %collective-permute-start.11 = (bf16[192,1024]{1,0:T(8,128)(2,1)}, bf16[192,1024]{1,0:T(8,128)(2,1)S(1)}, u32[]{:S(2)}, u32[]{:S(2)}) collective-permute-start(bf16[192,1024]{1,0:T(8,128)(2,1)} %get-tuple-element.9), channel_id=1, source_target_pairs={{0,0},{1,8},{8,1},{9,9},{16,16},{17,24},{24,17},{25,25},{2,2},{3,1... | collective-permute-start | bytes 1179656 | tf_op jit(solution)/shard_map/ppermute | solution.py:37
  107.9 38.4 %collective-permute-start.13 = (bf16[192,1024]{1,0:T(8,128)(2,1)}, bf16[192,1024]{1,0:T(8,128)(2,1)S(1)}, u32[]{:S(2)}, u32[]{:S(2)}) collective-permute-start(bf16[192,1024]{1,0:T(8,128)(2,1)} %get-tuple-element.10), channel_id=1, source_target_pairs={{0,1},{1,9},{8,16},{9,24},{16,17},{17,25},{24,0},{25,8},{2,3},{3,1... | collective-permute-start | bytes 1179656 | tf_op jit(solution)/shard_map/ppermute | solution.py:37
  110.4 36.0 %collective-permute-start.15 = (bf16[192,1024]{1,0:T(8,128)(2,1)}, bf16[192,1024]{1,0:T(8,128)(2,1)S(1)}, u32[]{:S(2)}, u32[]{:S(2)}) collective-permute-start(bf16[192,1024]{1,0:T(8,128)(2,1)} %get-tuple-element.11), channel_id=1, source_target_pairs={{0,16},{1,24},{8,17},{9,25},{16,0},{17,8},{24,1},{25,9},{2,18},{3,... | collective-permute-start | bytes 1179656 | tf_op jit(solution)/shard_map/ppermute | solution.py:37
  117.8 32.6 %collective-permute-start.17 = (bf16[192,1024]{1,0:T(8,128)(2,1)}, bf16[192,1024]{1,0:T(8,128)(2,1)S(1)}, u32[]{:S(2)}, u32[]{:S(2)}) collective-permute-start(bf16[192,1024]{1,0:T(8,128)(2,1)} %get-tuple-element.12), channel_id=1, source_target_pairs={{0,17},{1,25},{8,0},{9,8},{16,1},{17,9},{24,16},{25,24},{2,19},{3,... | collective-permute-start | bytes 1179656 | tf_op jit(solution)/shard_map/ppermute | solution.py:37
  117.8 17.3 %collective-permute-start.4 = (bf16[128,3072]{1,0:T(8,128)(2,1)}, bf16[128,3072]{1,0:T(8,128)(2,1)S(1)}, u32[]{:S(2)}, u32[]{:S(2)}) collective-permute-start(bf16[128,3072]{1,0:T(8,128)(2,1)} %collective-permute-done.3), channel_id=1, source_target_pairs={{0,1},{1,0},{2,3},{3,2},{4,5},{5,4},{6,7},{7,6},{8,9},{9,8},{10,11... | collective-permute-start | bytes 2359304 | tf_op jit(solution)/shard_map/ppermute | solution.py:48
  125.1 13.0 %collective-permute-start.6 = (bf16[128,3072]{1,0:T(8,128)(2,1)}, bf16[128,3072]{1,0:T(8,128)(2,1)S(1)}, u32[]{:S(2)}, u32[]{:S(2)}) collective-permute-start(bf16[128,3072]{1,0:T(8,128)(2,1)} %collective-permute-done.5), channel_id=1, source_target_pairs={{0,1},{1,0},{2,3},{3,2},{4,5},{5,4},{6,7},{7,6},{8,9},{9,8},{10,11... | collective-permute-start | bytes 2359304 | tf_op jit(solution)/shard_map/ppermute | solution.py:48
  135.1 17.3 %collective-permute-start.8 = (bf16[128,3072]{1,0:T(8,128)(2,1)}, bf16[128,3072]{1,0:T(8,128)(2,1)S(1)}, u32[]{:S(2)}, u32[]{:S(2)}) collective-permute-start(bf16[128,3072]{1,0:T(8,128)(2,1)} %collective-permute-done.7), channel_id=1, source_target_pairs={{0,1},{1,0},{2,3},{3,2},{4,5},{5,4},{6,7},{7,6},{8,9},{9,8},{10,11... | collective-permute-start | bytes 2359304 | tf_op jit(solution)/shard_map/ppermute | solution.py:48
  138.2 22.9 %collective-permute-start.10 = (bf16[128,3072]{1,0:T(8,128)(2,1)}, bf16[128,3072]{1,0:T(8,128)(2,1)S(1)}, u32[]{:S(2)}, u32[]{:S(2)}) collective-permute-start(bf16[128,3072]{1,0:T(8,128)(2,1)} %collective-permute-done.9), channel_id=1, source_target_pairs={{0,1},{1,0},{2,3},{3,2},{4,5},{5,4},{6,7},{7,6},{8,9},{9,8},{10,11... | collective-permute-start | bytes 2359304 | tf_op jit(solution)/shard_map/ppermute | solution.py:48
  146.4 7.1 %collective-permute-start.12 = (bf16[192,1024]{1,0:T(8,128)(2,1)S(1)}, bf16[192,1024]{1,0:T(8,128)(2,1)S(1)}, u32[]{:S(2)}, u32[]{:S(2)}) collective-permute-start(bf16[192,1024]{1,0:T(8,128)(2,1)S(1)} %collective-permute-done.11), channel_id=1, source_target_pairs={{0,1},{1,0},{2,3},{3,2},{4,5},{5,4},{6,7},{7,6},{8,9},{9,8},{10,11... | collective-permute-start | bytes 1179656 | tf_op jit(solution)/shard_map/ppermute | solution.py:48
  146.4 8.6 %collective-permute-start.14 = (bf16[192,1024]{1,0:T(8,128)(2,1)S(1)}, bf16[192,1024]{1,0:T(8,128)(2,1)S(1)}, u32[]{:S(2)}, u32[]{:S(2)}) collective-permute-start(bf16[192,1024]{1,0:T(8,128)(2,1)S(1)} %collective-permute-done.13), channel_id=1, source_target_pairs={{0,1},{1,0},{2,3},{3,2},{4,5},{5,4},{6,7},{7,6},{8,9},{9,8},{10,11... | collective-permute-start | bytes 1179656 | tf_op jit(solution)/shard_map/ppermute | solution.py:48
  150.4 6.2 %collective-permute-start.16 = (bf16[192,1024]{1,0:T(8,128)(2,1)S(1)}, bf16[192,1024]{1,0:T(8,128)(2,1)S(1)}, u32[]{:S(2)}, u32[]{:S(2)}) collective-permute-start(bf16[192,1024]{1,0:T(8,128)(2,1)S(1)} %collective-permute-done.15), channel_id=1, source_target_pairs={{0,1},{1,0},{2,3},{3,2},{4,5},{5,4},{6,7},{7,6},{8,9},{9,8},{10,11... | collective-permute-start | bytes 1179656 | tf_op jit(solution)/shard_map/ppermute | solution.py:48
  152.5 5.7 %collective-permute-start.18 = (bf16[192,1024]{1,0:T(8,128)(2,1)S(1)}, bf16[192,1024]{1,0:T(8,128)(2,1)S(1)}, u32[]{:S(2)}, u32[]{:S(2)}) collective-permute-start(bf16[192,1024]{1,0:T(8,128)(2,1)S(1)} %collective-permute-done.17), channel_id=1, source_target_pairs={{0,1},{1,0},{2,3},{3,2},{4,5},{5,4},{6,7},{7,6},{8,9},{9,8},{10,11... | collective-permute-start | bytes 1179656 | tf_op jit(solution)/shard_map/ppermute | solution.py:48
  175.0 24.8 %all-to-all-start.1 = ((bf16[8,96,1024]{2,1,0:T(8,128)(2,1)}), bf16[8,96,1024]{2,1,0:T(8,128)(2,1)S(1)}, u32[]{:S(2)}, u32[]{:S(2)}) async-start(bf16[8,96,1024]{2,1,0:T(8,128)(2,1)} %bitcast.166), calls=%async_computation.1 | async-start | bytes 3145728 | tf_op jit(solution)/shard_map/all_to_all | solution.py:136
  (11 other events, 54.5 us)
